TPU v7x, 256 devices: a whole 4x4x8 slice. The times are simulated.
256 devices in a mesh: cfg: 2 (over y_hi), uly: 8 (over x, core), blk: 16 (over y_lo, z).
Axes of the slice: x: 4, y: 4 (y_hi: 2, y_lo: 2; y = y_hi * 2 + y_lo), z: 8, core: 2. Of those that a mesh axis runs over, the one named last changes fastest.
Arguments:
- hidden: bfloat16 [2, 8192, 3072], P('cfg', ('uly', 'blk')), may hold values from -400 to 400
- final_mod: float32 [2, 2, 3072], P('cfg'), may hold values from -3 to 3
- final_weight: bfloat16 [3072, 64], replicated, may hold values from -0.109375 to 0.109375
- latent: float32 [8192, 64], P(('uly', 'blk')), may hold values from -6 to 6
- guidance: float32 [50], replicated, may hold values from 2 to 6
- step_size: float32 [50], replicated, may hold values from 0.1 to 0.4
- step_index: int32 [1], replicated, may hold values from 0 to 49
- embed_weight: float32 [64, 3072], replicated, may hold values from -0.75 to 0.75
- block_mod: float32 [2, 2, 3072], P('cfg'), may hold values from -3 to 3
- qkv_weight: bfloat16 [3072, 3, 3072], P(None, None, 'uly'), may hold values from -0.109375 to 0.109375
- qk_gains: float32 [2, 128], replicated, may hold values from 0.25 to 1.75
Outputs:
- next_latent: float32 [8192, 64], P(('uly', 'blk'))
- attention: bfloat16 [2, 8192, 3072], P('cfg', ('uly', 'blk'))
Inputs may be any that keep to these rules, and one draw needn't show every extreme that they name: `step_index`: index of the current denoising step.
All inputs are finite; a program needn't handle non-finite values.
Results may differ from a plain program's by a relative error of at most 0.007.
Values may be sent and summed in bfloat16 or wider, within the bound.
A program may use at most 128 MiB of HBM per device.

v0:
```python
import jax
import jax.numpy as jnp
from jax import lax
from jax.sharding import PartitionSpec as P

HEAD_DIM = 128
GRID_H = 32
GRID_W = 32


def from_partner(shard, axis, stride):
    return lax.ppermute(shard, axis, [(i, i ^ 1 << stride) for i in range(lax.axis_size(axis))])


def layer_norm(rows):
    mean = jnp.mean(rows, axis=-1, keepdims=True)
    centred = rows - mean
    var = jnp.mean(centred * centred, axis=-1, keepdims=True)
    return centred * lax.rsqrt(var + 1e-06)


def modulate(rows, mod):
    return layer_norm(rows) * (1.0 + mod[1]) + mod[0]


def rms_scale(values, gain):
    power = jnp.mean(values * values, axis=-1, keepdims=True)
    return values * lax.rsqrt(power + 1e-06) * gain


def axis_angles(coord, width):
    exponents = jnp.arange(0, width, 2).astype(jnp.float32) / width
    freqs = 1.0 / 256.0**exponents
    return coord.astype(jnp.float32)[:, None] * freqs[None, :]


def rope_angles(positions):
    time_dim = HEAD_DIM // 8
    space_dim = (HEAD_DIM - time_dim) // 2
    frame = positions // (GRID_H * GRID_W)
    row_pos = positions // GRID_W % GRID_H
    col_pos = positions % GRID_W
    return jnp.concatenate(
        [
            axis_angles(frame, time_dim),
            axis_angles(row_pos, space_dim),
            axis_angles(col_pos, space_dim),
        ],
        axis=-1,
    )


def apply_rope(values, angles):
    count, heads, width = values.shape
    pairs = values.reshape(count, heads, width // 2, 2)
    first = pairs[..., 0]
    second = pairs[..., 1]
    cosine = jnp.cos(angles)[:, None, :]
    sine = jnp.sin(angles)[:, None, :]
    rotated = jnp.stack([first * cosine - second * sine, first * sine + second * cosine], axis=-1)
    return rotated.reshape(count, heads, width)


def group_positions(length, rows):
    gathered_row = jnp.arange(length, dtype=jnp.int32)
    blocks = lax.axis_size("blk")
    own_block = lax.axis_index("blk")
    return gathered_row // rows * (blocks * rows) + own_block * rows + gathered_row % rows


def project_heads(normed, qkv_weight, qk_gains, angles):
    mixed = jnp.einsum("rd,dtc->rtc", normed, qkv_weight, preferred_element_type=jnp.float32)
    count = mixed.shape[0]
    width = mixed.shape[2]
    split = mixed.reshape(count, 3, width // HEAD_DIM, HEAD_DIM)
    query = apply_rope(rms_scale(split[:, 0], qk_gains[0]), angles)
    key_part = apply_rope(rms_scale(split[:, 1], qk_gains[1]), angles)
    stacked = jnp.stack([query, key_part, split[:, 2]], axis=1)
    return stacked.reshape(count, 3, width).astype(jnp.bfloat16)


def attend_block(carry, queries, keys, values):
    numer, total = carry
    scores = jnp.einsum(
        "qhd,khd->hqk", queries, keys, preferred_element_type=jnp.float32
    ) * HEAD_DIM ** (-0.5)
    weights = jnp.exp(scores)
    total = total + jnp.sum(weights, axis=-1)
    numer = numer + jnp.einsum(
        "hqk,khd->qhd", weights.astype(jnp.bfloat16), values, preferred_element_type=jnp.float32
    )
    return (numer, total)


def on_device(
    hidden,
    final_mod,
    final_weight,
    latent,
    guidance,
    step_size,
    step_index,
    embed_weight,
    block_mod,
    qkv_weight,
    qk_gains,
):
    rows = latent.shape[0]
    chosen = (jnp.arange(guidance.shape[0], dtype=jnp.int32) == step_index[0]).astype(jnp.float32)
    scale_now = jnp.sum(chosen * guidance)
    step_now = jnp.sum(chosen * step_size)
    final_rows = modulate(hidden[0].astype(jnp.float32), final_mod[0]).astype(jnp.bfloat16)
    velocity = jnp.dot(final_rows, final_weight, preferred_element_type=jnp.float32)
    partner = from_partner(velocity, "cfg", 0)
    leading = lax.axis_index("cfg") == 0
    cond_part = jnp.where(leading, velocity, partner)
    uncond_part = jnp.where(leading, partner, velocity)
    next_latent = latent - step_now * (uncond_part + scale_now * (cond_part - uncond_part))
    embedded = jnp.dot(next_latent, embed_weight, precision=lax.Precision.HIGHEST)
    normed = modulate(embedded, block_mod[0]).astype(jnp.bfloat16)
    piece = lax.all_gather(normed, "uly", axis=0, tiled=True)
    angles = rope_angles(group_positions(piece.shape[0], rows))
    projected = project_heads(piece, qkv_weight, qk_gains, angles)
    count = projected.shape[0]
    width = projected.shape[2]
    local_heads = width // HEAD_DIM
    queries = projected[:, 0].reshape(count, local_heads, HEAD_DIM)
    key_values = projected[:, 1:]
    start_carry = (
        jnp.zeros((count, local_heads, HEAD_DIM), jnp.float32),
        jnp.zeros((local_heads, count), jnp.float32),
    )
    carry = start_carry
    piece = lax.all_gather(key_values, "blk", axis=0, tiled=True)
    length = piece.shape[0]
    blocks = piece.reshape(length // 512, 512, 2, local_heads, HEAD_DIM)

    def step_block(state, block):
        return (attend_block(state, queries, block[:, 0], block[:, 1]), None)

    carry, unused = lax.scan(step_block, carry, blocks)
    numer, total = carry
    result = (numer / jnp.transpose(total)[:, :, None]).reshape(count, width).astype(jnp.bfloat16)
    attention = lax.all_to_all(result, "uly", split_axis=0, concat_axis=1, tiled=True)
    return (next_latent, attention[None])


def solution(mesh):
    return jax.shard_map(
        on_device,
        mesh=mesh,
        in_specs=(
            P("cfg", ("uly", "blk"), None),
            P("cfg", None, None),
            P(),
            P(("uly", "blk"), None),
            P(),
            P(),
            P(),
            P(),
            P("cfg", None, None),
            P(None, None, "uly"),
            P(),
        ),
        out_specs=(P(("uly", "blk"), None), P("cfg", ("uly", "blk"), None)),
        check_vma=False,
    )
```

profile of v0, /device:TPU:1, one launch (start us, length us, event | category | flops | bytes accessed | tf_op | source)
XLA Modules:
  0.0 371.3 jit_solution(8050242641679524291)
XLA Ops:
  12.0 3.8 %collective-permute-start = (f32[64,64]{1,0:T(8,128)S(1)}, f32[64,64]{1,0:T(8,128)S(1)}, u32[]{:S(2)}, u32[]{:S(2)}) collective-permute-start(f32[64,64]{1,0:T(8,128)S(1)} %fusion.15), channel_id=1, source_target_pairs={{0,128},{128,0},{1,129},{129,1},{2,130},{130,2},{3,131},{131,3},{4... | collective-permute-start | bytes 49160 | tf_op jit(solution)/shard_map/ppermute | solution.py:12
  18.7 2.1 multiply_subtract_fusion
  24.8 32.2 %all-gather.3.cloned.1.call-done = bf16[512,3072]{1,0:T(8,128)(2,1)} async-done(((bf16[64,3072]{1,0:T(8,128)(2,1)}), bf16[512,3072]{1,0:T(8,128)(2,1)}) %all-gather.3.cloned.1.call-update) | async-done | bytes 3145744 | tf_op jit(solution)/shard_map/all_gather | solution.py:121
  57.0 7.2 %fusion.6 = f32[512,3,384]{0,2,1:T(8,128)S(1)} fusion(bf16[3072,3,384]{2,0,1:T(8,128)(2,1)} %param.22, bf16[512,3072]{1,0:T(8,128)(2,1)} %all-gather.3.cloned.1.call-done), kind=kOutput, calls=%fused_computation.13 | convolution fusion | flops 3623878656 | bytes 12582912 | tf_op jit(solution)/shard_map/rd,dtc->rtc/dot_general | solution.py:72
  66.2 2.1 subtract_convert_fusion
  71.7 141.6 %all-gather.5.cloned.1.call-done = bf16[8192,2,384]{0,2,1:T(8,128)(2,1)} async-done(((bf16[512,2,384]{0,2,1:T(8,128)(2,1)}), bf16[8192,2,384]{0,2,1:T(8,128)(2,1)}) %all-gather.5.cloned.1.call-update) | async-done | bytes 12582928 | tf_op jit(solution)/shard_map/all_gather | solution.py:134
  213.3 12.8 %copy.35 = bf16[96,8,16,512]{3,2,1,0:T(8,128)(2,1)} copy(bf16[96,8,16,512]{3,1,2,0:T(8,128)(2,1)} %bitcast.90) | data formatting | bytes 25165824
  226.1 17.6 %copy.28 = bf16[16,512,2,3,128]{4,1,3,2,0:T(8,128)(2,1)} copy(bf16[16,512,2,3,128]{1,0,4,3,2:T(8,128)(2,1)} %bitcast.89) | data formatting | bytes 25165824
  243.8 104.7 %while.13 = (s32[]{:T(128)}, f32[512,3,128]{0,2,1:T(8,128)}, f32[3,512]{1,0:T(4,128)S(1)}, bf16[16,512,2,3,128]{4,1,3,2,0:T(8,128)(2,1)}, bf16[512,3,128]{2,0,1:T(8,128)(2,1)S(1)}, /*index=5*/s32[]{:T(128)}, s32[]{:T(128)}) while((s32[]{:T(128)}, f32[512,3,128]{0,2,1:T(8,128)}, f32[3,512]{1,0:T(4,128)S(1)}, ...), condition=%wide.region_10.11_spmd.clone, body=%wide.region_8.10_spmd.clone.sunk | while | flops 406193664 | bytes 10641500 | solution.py:141
  243.8 2.1 dynamic-slice_bitcast_fusion.2
  247.5 2.5 fusion.49
  250.1 2.1 dynamic-slice_bitcast_fusion.2
  253.8 2.8 fusion.49
  256.6 2.1 dynamic-slice_bitcast_fusion.2
  258.7 1.6 bitcast_reduce_fusion.2
  260.3 2.8 fusion.49
  263.2 2.1 dynamic-slice_bitcast_fusion.2
  265.3 1.6 bitcast_reduce_fusion.2
  266.9 2.8 fusion.49
  269.7 2.1 dynamic-slice_bitcast_fusion.2
  271.8 1.6 bitcast_reduce_fusion.2
  273.5 2.8 fusion.49
  276.3 2.1 dynamic-slice_bitcast_fusion.2
  278.4 1.6 bitcast_reduce_fusion.2
  280.0 2.8 fusion.49
  282.8 2.1 dynamic-slice_bitcast_fusion.2
  285.0 1.6 bitcast_reduce_fusion.2
  286.6 2.8 fusion.49
  289.4 2.1 dynamic-slice_bitcast_fusion.2
  291.5 1.6 bitcast_reduce_fusion.2
  293.1 2.8 fusion.49
  296.0 2.1 dynamic-slice_bitcast_fusion.2
  299.7 2.8 fusion.49
  302.5 2.1 dynamic-slice_bitcast_fusion.2
  306.3 2.8 fusion.49
  309.1 2.1 dynamic-slice_bitcast_fusion.2
  312.8 2.8 fusion.49
  315.6 2.1 dynamic-slice_bitcast_fusion.2
  319.4 2.8 fusion.49
  322.2 2.1 dynamic-slice_bitcast_fusion.2
  325.9 2.8 fusion.49
  328.8 2.1 dynamic-slice_bitcast_fusion.2
  332.5 2.8 fusion.49
  335.3 2.1 dynamic-slice_bitcast_fusion.2
  339.1 2.8 fusion.49
  341.9 2.1 dynamic-slice_bitcast_fusion.2
  345.6 2.8 fusion.49
  350.4 12.8 %all_to_all.13 = bf16[8,64,384]{2,1,0:T(8,128)(2,1)S(1)} all-to-all(bf16[8,64,384]{2,1,0:T(8,128)(2,1)S(1)} %convert_element_type.72), channel_id=1, replica_groups=mesh['cfg'=2,'uly'=8,'blk'=16] {'uly'}, dimensions={0} | all-to-all | bytes 786432 | tf_op jit(solution)/shard_map/all_to_all | solution.py:144
  (83 shorter events, 35.5 us)
Async XLA Ops:
  7.2 14.3 %copy-start = (f32[64,3072]{1,0:T(8,128)S(1)}, f32[64,3072]{1,0:T(8,128)}, u32[]{:S(2)}) copy-start(f32[64,3072]{1,0:T(8,128)} %param.20) | copy-start | bytes 2359300
  7.2 49.9 %all-gather.3.cloned.1.call-start = ((), (), s32[]{:S(2)}) async-start(), calls=%async_computation.1 | async-start | bytes 3538944 | tf_op jit(solution)/shard_map/all_gather | solution.py:121
  8.1 15.7 %copy-start.3 = (f32[2,128]{1,0:T(2,128)S(1)}, f32[2,128]{1,0:T(2,128)}, u32[]{:S(2)}) copy-start(f32[2,128]{1,0:T(2,128)} %param.23) | copy-start | bytes 3076
  12.0 6.7 %collective-permute-start = (f32[64,64]{1,0:T(8,128)S(1)}, f32[64,64]{1,0:T(8,128)S(1)}, u32[]{:S(2)}, u32[]{:S(2)}) collective-permute-start(f32[64,64]{1,0:T(8,128)S(1)} %fusion.15), channel_id=1, source_target_pairs={{0,128},{128,0},{1,129},{129,1},{2,130},{130,2},{3,131},{131,3},{4... | collective-permute-start | bytes 49160 | tf_op jit(solution)/shard_map/ppermute | solution.py:12
  20.8 0.6 copy-start.2
  23.6 189.7 %all-gather.5.cloned.1.call-start = ((), (), s32[]{:S(2)}) async-start(), calls=%async_computation.2 | async-start | bytes 13369344 | tf_op jit(solution)/shard_map/all_gather | solution.py:134
  348.4 16.0 %copy-start.1 = (f32[64,3072]{1,0:T(8,128)S(1)}, f32[64,3072]{1,0:T(8,128)}, u32[]{:S(2)}) copy-start(f32[64,3072]{1,0:T(8,128)} %param.20) | copy-start | bytes 2359300
Sparse Core Ops, SparseCore 0:
  23.7 33.3 all-gather.2
  70.5 142.7 all-gather.4
where the time goes:
time: 374 us; the launch traced here: 371 us
  waiting for transfers between devices  174 us (47%)
  matrix products  79.8 us (21%)
  local copies, waits for them, and re-layouts  68.5 us (18%)
  other arithmetic  16.8 us (4%)
  between operations  15 us (4%)
  blocking collectives  12.8 us (3%)
  starting transfers between devices  4.09 us (1%)
    all_gather x1, waiting for transfers between devices, on_device(): piece = lax.all_gather(key_values, 'blk', axis=0, tiled=True)  142 us
    dot_general x16, matrix products, attend_block(): jnp.einsum('hqk,khd->qhd', weights.astype(jnp.bfloat16), values, preferre...  44.7 us
    squeeze x16, local copies, waits for them, and re-layouts, on_device(): carry, unused = lax.scan(step_block, carry, blocks)  33.8 us
    all_gather x1, waiting for transfers between devices, on_device(): piece = lax.all_gather(normed, 'uly', axis=0, tiled=True)  32.2 us
    unnamed x11, local copies, waits for them, and re-layouts  31.3 us
    dot_general x16, matrix products, attend_block(): jnp.einsum('qhd,khd->hqk', queries, keys, preferred_element_type=jnp.floa...  25.6 us
    all_to_all x1, blocking collectives, on_device(): lax.all_to_all(result, 'uly', split_axis=0, concat_axis=1, tiled=True)  12.8 us
  transfers between devices with their start and end apart: 3, of which 2 were waited for; matrix products, arithmetic and copies ran while one was open for 1% of the time, Pallas kernels for 0%

commit v1 on v0

v1 whole, which is shorter than its diff:
```python
import functools
import math

import jax
import jax.numpy as jnp
import numpy as np
from jax import lax
from jax.experimental import pallas as pl
from jax.experimental.pallas import tpu as pltpu
from jax.sharding import PartitionSpec as P

HEAD_DIM = 128
GRID_H = 32
GRID_W = 32
CHAN = 64
EPS = 1e-6
MESH = pl.DeviceIdType.MESH
F32 = jnp.float32
BF16 = jnp.bfloat16


def pair_angles():
    time_dim = HEAD_DIM // 8
    space_dim = (HEAD_DIM - time_dim) // 2
    out = []
    for coords, width in ((8, time_dim), (GRID_H, space_dim), (GRID_W, space_dim)):
        freqs = 1.0 / 256.0 ** (np.arange(0, width, 2) / width)
        out.append(np.arange(coords)[:, None] * freqs[None, :])
    return out


def rope_tables():
    time, row, col = pair_angles()
    frames = time.shape[0]
    blocks = GRID_H // 2
    key = np.zeros((64, 2, blocks, GRID_W))
    query = np.zeros((blocks, 64, 2, 2, GRID_W))
    for half in range(2):
        for b in range(blocks):
            key[8:36, half, b] = row[2 * b + half][:, None]
            key[36:64, half, b] = col.T
            query[b, 8:36, :, half] = row[2 * b + half][:, None, None]
            query[b, 36:64, :, half] = col.T[:, None]
    key = key.reshape(64, 2 * blocks * GRID_W)
    query = query.reshape(blocks, 64, 128)
    query_time = np.repeat(time.T, 64, axis=1)
    key_time = np.repeat(time[:, :, None], 128, axis=2)

    def both(angles, axis):
        return np.stack([np.cos(angles), np.sin(angles)], axis=axis).astype(np.float32)

    return both(key, 0), both(key_time, 1), both(query, 1), both(query_time, 0)


def mm(a, b):
    return jnp.dot(a, b, preferred_element_type=F32)


def mm_nt(a, b, precision=None):
    return lax.dot_general(a, b, (((1,), (1,)), ((), ())), precision=precision, preferred_element_type=F32)


def split_bf16(value):
    high = value.astype(BF16)
    return high, (value - high.astype(F32)).astype(BF16)


def kernel(
    n_uly,
    n_blk,
    guid_s,
    size_s,
    index_s,
    hidden_h,
    fmod_h,
    fw_h,
    latent_h,
    embed_h,
    bmod_h,
    w_h,
    gains_v,
    ktab_h,
    ktime_h,
    qtab_h,
    qtime_h,
    next_ref,
    out_ref,
    hidden_v,
    fmod_v,
    fw_v,
    latent_v,
    embed_v,
    bmod_v,
    w_v,
    ktab_v,
    ktime_v,
    qtab_v,
    qtime_v,
    vel_mine,
    vel_other,
    xp_v,
    xq_v,
    lhs_v,
    tk_v,
    tq_v,
    sv_v,
    tab_v,
    aug_v,
    kt_v,
    q_v,
    acc_v,
    stage_v,
    load_sem,
    vel_send,
    vel_recv,
    blk_send,
    blk_recv,
    uly_send,
    uly_recv,
    x_send,
    x_recv,
    sib_send,
    sib_recv,
    out_send,
    out_recv,
    own_sem,
):
    cfg = lax.axis_index("cfg")
    uly = lax.axis_index("uly")
    blk = lax.axis_index("blk")
    x_at = uly // 2
    core = uly % 2
    sib = uly + 1 - 2 * core
    n_x = n_uly // 2

    def remote(src, dst, send, recv, device):
        return pltpu.make_async_remote_copy(
            src_ref=src, dst_ref=dst, send_sem=send, recv_sem=recv, device_id=device, device_id_type=MESH
        )

    pairs = [
        (hidden_h, hidden_v),
        (fmod_h, fmod_v),
        (fw_h, fw_v),
        (latent_h, latent_v),
        (embed_h, embed_v),
        (bmod_h, bmod_v),
        (w_h.at[0], w_v.at[0]),
        (w_h.at[1], w_v.at[1]),
        (w_h.at[2], w_v.at[2]),
        (ktab_h, ktab_v),
        (ktime_h, ktime_v),
        (qtab_h.at[blk], qtab_v),
        (qtime_h, qtime_v),
    ]
    loads = [pltpu.make_async_copy(s, d, load_sem.at[i]) for i, (s, d) in enumerate(pairs)]
    for load in loads:
        load.start()

    barrier = pltpu.get_barrier_semaphore()
    pl.semaphore_signal(barrier, inc=1, device_id=(1 - cfg, uly, blk), device_id_type=MESH)
    for d in range(1, n_blk):
        pl.semaphore_signal(barrier, inc=1, device_id=(cfg, uly, (blk + d) % n_blk), device_id_type=MESH)
    for d in range(1, n_uly):
        pl.semaphore_signal(barrier, inc=1, device_id=(cfg, (uly + d) % n_uly, blk), device_id_type=MESH)

    for i in range(3):
        loads[i].wait()
    rows = hidden_v[...].astype(F32)
    mean = jnp.mean(rows, axis=1, keepdims=True)
    rows = rows - mean
    var = jnp.mean(rows * rows, axis=1, keepdims=True)
    rows = rows * lax.rsqrt(var + EPS)
    rows = (rows * (1.0 + fmod_v[1:2, :]) + fmod_v[0:1, :]).astype(BF16)
    vel = mm_nt(rows, fw_v[...])
    vel_mine[...] = jnp.concatenate([vel[0:32], vel[32:64]], axis=1)
    pl.semaphore_wait(barrier, n_blk + n_uly - 1)
    vel_copy = remote(vel_mine, vel_other, vel_send, vel_recv, (1 - cfg, uly, blk))
    vel_copy.start()

    loads[3].wait()
    loads[4].wait()
    loads[5].wait()
    emb = embed_v[...]
    emb = emb - jnp.mean(emb, axis=1, keepdims=True)
    high, low = split_bf16(emb)
    stack = jnp.concatenate([high, low], axis=0)
    gram = mm_nt(stack, stack)
    gram = (gram[0:64, 0:64] + gram[0:64, 64:128] + gram[64:128, 0:64] + gram[64:128, 64:128]) * (1.0 / emb.shape[1])
    high, low = split_bf16(emb * (1.0 + bmod_v[1:2, :]))
    lhs_v[0:64, :] = high
    lhs_v[64:128, :] = low
    high, low = split_bf16(bmod_v[0:1, :])
    lhs_v[128:144, :] = jnp.concatenate([high, low, jnp.zeros((14, high.shape[1]), BF16)], axis=0)

    step = index_s[0]
    scale_now = guid_s[step]
    step_now = size_s[step]
    vel_copy.wait()
    mine = vel_mine[...]
    other = vel_other[...]
    cond = jnp.where(cfg == 0, mine, other)
    uncond = jnp.where(cfg == 0, other, mine)
    guided = uncond + scale_now * (cond - uncond)
    guided = jnp.concatenate([guided[:, 0:64], guided[:, 64:128]], axis=0)
    latent = latent_v[...] - step_now * guided
    next_ref[...] = latent
    power = jnp.dot(latent, gram, precision=lax.Precision.HIGHEST, preferred_element_type=F32)
    var = jnp.maximum(jnp.sum(power * latent, axis=1, keepdims=True), 0.0)
    normed = (latent * lax.rsqrt(var + EPS)).astype(BF16)
    packed = jnp.concatenate([normed[0:32], normed[32:64]], axis=1)
    own_rows = pl.ds(pl.multiple_of(blk * 32, 32), 32)
    xp_v[uly, own_rows, :] = packed
    xq_v[uly] = packed

    blk_copies = []
    for d in range(1, n_blk):
        there = xp_v.at[uly, own_rows, :]
        blk_copies.append(
            remote(there, there, blk_send.at[d - 1], blk_recv.at[d - 1], (cfg, uly, (blk + d) % n_blk))
        )
    uly_copies = []
    for d in range(1, n_uly):
        there = xq_v.at[uly]
        uly_copies.append(
            remote(there, there, uly_send.at[d - 1], uly_recv.at[d - 1], (cfg, (uly + d) % n_uly, blk))
        )
    for copy in blk_copies + uly_copies:
        copy.start()

    lanes = lax.broadcasted_iota(jnp.int32, (128, 128), 1)
    sublanes = lax.broadcasted_iota(jnp.int32, (128, 128), 0)
    source = jnp.where(sublanes < 64, 2 * sublanes, 2 * sublanes - 127)
    perm = jnp.where(lanes == source, 1.0, 0.0)
    perm_b = perm.astype(BF16)
    lhs = lhs_v[...]
    for j in range(3):
        loads[6 + j].wait()
        full = mm(lhs, w_v[j])
        weight = full[0:64] + full[64:128]
        bias = full[128:129] + full[129:130]
        square = jnp.concatenate([weight, bias, jnp.zeros((63, weight.shape[1]), F32)], axis=0)
        high, low = split_bf16(square)
        for h in range(3):
            cols = slice(h * 128, h * 128 + 128)
            if j == 2:
                sv_v[h, 0:128, :] = high[:, cols]
                sv_v[h, 128:256, :] = low[:, cols]
            else:
                target = tq_v if j == 0 else tk_v
                target[cols, 0:128] = mm_nt(perm_b, high[:, cols]).astype(BF16)
                target[cols, 128:256] = mm_nt(perm_b, low[:, cols]).astype(BF16)

    for i in range(9, 13):
        loads[i].wait()
    gains = jnp.concatenate([gains_v[...], jnp.zeros((6, 128), F32)], axis=0)
    gains = mm_nt(perm, gains, precision=lax.Precision.HIGHEST)
    ga_q = gains[0:64, 0:1] * (math.log2(math.e) / math.sqrt(HEAD_DIM))
    gb_q = gains[64:128, 0:1] * (math.log2(math.e) / math.sqrt(HEAD_DIM))
    ga_k = gains[0:64, 1:2]
    gb_k = gains[64:128, 1:2]
    cosine, sine = ktab_v[0], ktab_v[1]
    tab_v[0] = ga_k * cosine
    tab_v[1] = gb_k * sine
    tab_v[2] = ga_k * sine
    tab_v[3] = gb_k * cosine
    ga_t = jnp.broadcast_to(ga_k[0:8], (8, 128))
    gb_t = jnp.broadcast_to(gb_k[0:8], (8, 128))

    one_hot = jnp.where(lax.broadcasted_iota(jnp.int32, (1, 128), 1) == 64, 1.0, 0.0)
    low_lanes = lax.broadcasted_iota(jnp.int32, (1, 128), 1) < 64

    def unpack(value):
        wide = value.astype(F32)
        first = jnp.where(low_lanes, wide, one_hot).astype(BF16)
        second = jnp.where(low_lanes, pltpu.roll(wide, 64, 1), one_hot).astype(BF16)
        return first, second

    def rotate(proj, t1, t2, t3, t4):
        a, b = proj[0:64], proj[64:128]
        power = jnp.sum(a * a + b * b, axis=0, keepdims=True) * (1.0 / HEAD_DIM)
        scale = lax.rsqrt(power + EPS)
        return (a * t1 - b * t2) * scale, (a * t3 + b * t4) * scale

    def make_keys(chunk, slot):
        cos_t, sin_t = ktime_v[chunk, 0], ktime_v[chunk, 1]
        for i, row in enumerate((ga_t * cos_t, gb_t * sin_t, ga_t * sin_t, gb_t * cos_t)):
            tab_v[i, 0:8, :] = jnp.concatenate([row] * 8, axis=1)
        halves = unpack(xp_v[chunk])
        for half in range(2):
            cols = slice(half * 512, half * 512 + 512)
            aug_v[slot, cols, :] = halves[half]
            proj = mm_nt(tk_v[...], jnp.concatenate([halves[half]] * 2, axis=1))
            tabs = [tab_v[i, :, cols] for i in range(4)]
            for h in range(3):
                ka, kb = rotate(proj[h * 128 : h * 128 + 128], *tabs)
                kt_v[slot, h, 0:64, cols] = ka.astype(BF16)
                kt_v[slot, h, 64:128, cols] = kb.astype(BF16)

    def blk_from(d):
        there = xp_v.at[uly, pl.ds(pl.multiple_of((blk + n_blk - d) % n_blk * 32, 32), 32), :]
        return remote(there, there, blk_send.at[d - 1], blk_recv.at[d - 1], (cfg, uly, (blk + d) % n_blk))

    for d in range(1, n_blk):
        blk_from(d).wait_recv()

    def x_copy(d, slot):
        there = xp_v.at[slot]
        return remote(there, there, x_send.at[d - 1], x_recv.at[d - 1], (cfg, (x_at + d) % n_x * 2 + core, blk))

    def sib_copy(d, slot):
        there = xp_v.at[slot]
        return remote(there, there, sib_send.at[d], sib_recv.at[d], (cfg, sib, blk))

    def x_slot(d):
        return (x_at + n_x - d) % n_x * 2 + core

    def x_slot_sib(d):
        return (x_at + n_x - d) % n_x * 2 + 1 - core

    for d in (1, 3, 2):
        x_copy(d, uly).start()
    sib_copy(0, uly).start()

    for d in range(1, n_uly):
        there = xq_v.at[(uly + n_uly - d) % n_uly]
        remote(there, there, uly_send.at[d - 1], uly_recv.at[d - 1], (cfg, uly, blk)).wait_recv()
    parts = []
    for u in range(n_uly):
        parts += list(unpack(xq_v[u]))
    rows_q = jnp.concatenate(parts, axis=0)
    proj = mm_nt(tq_v[...], jnp.concatenate([rows_q, rows_q], axis=1))
    cos_q = jnp.concatenate([qtime_v[0], jnp.concatenate([qtab_v[0, 8:64]] * 4, axis=1)], axis=0)
    sin_q = jnp.concatenate([qtime_v[1], jnp.concatenate([qtab_v[1, 8:64]] * 4, axis=1)], axis=0)
    tabs = (ga_q * cos_q, gb_q * sin_q, ga_q * sin_q, gb_q * cos_q)
    for h in range(3):
        qa, qb = rotate(proj[h * 128 : h * 128 + 128], *tabs)
        q_v[h] = jnp.transpose(jnp.concatenate([qa, qb], axis=0)).astype(BF16)

    make_keys(uly, 0)
    acc_v[...] = jnp.zeros_like(acc_v)

    def attend(h, slot):
        scores = mm(q_v[h], kt_v[slot, h])
        return mm(jnp.exp2(scores).astype(BF16), aug_v[slot])

    def frame_of(r):
        d = jnp.where(r < 2, 0, jnp.where(r >= 6, 2, jnp.where(r % 2 == 0, 1, 3)))
        other = jnp.where(r < 4, jnp.where(r == 1, 1, 0), jnp.where(r < 6, 1, r % 2))
        at = (x_at + n_x - d) % n_x
        return at * 2 + jnp.where(other == 1, 1 - core, core)

    def body(r, _):
        slot = r % 2

        @pl.when(r == 0)
        def _():
            sib_copy(0, sib).wait_recv()

        @pl.when(r == 1)
        def _():
            x_copy(1, x_slot(1)).wait_recv()
            sib_copy(1, x_slot(1)).start()

        @pl.when(r == 2)
        def _():
            x_copy(3, x_slot(3)).wait_recv()
            sib_copy(3, x_slot(3)).start()

        @pl.when(r == 3)
        def _():
            sib_copy(1, x_slot_sib(1)).wait_recv()

        @pl.when(r == 4)
        def _():
            sib_copy(3, x_slot_sib(3)).wait_recv()
            x_copy(2, x_slot(2)).wait_recv()
            sib_copy(2, x_slot(2)).start()

        @pl.when(r == 6)
        def _():
            sib_copy(2, x_slot_sib(2)).wait_recv()

        make_keys(frame_of(r + 1), 1 - slot)
        for h in range(3):
            acc_v[h] += attend(h, slot)
        return 0

    lax.fori_loop(0, n_uly - 1, body, 0)

    def out_copy(h, d):
        to = (uly + d) % n_uly
        src = stage_v.at[h, pl.ds(pl.multiple_of(to * 64, 64), 64), :]
        dst = out_ref.at[:, pl.ds(pl.multiple_of((uly * 3 + h) * 128, 128), 128)]
        return remote(src, dst, out_send.at[h, d - 1], out_recv.at[h, d - 1], (cfg, to, blk))

    def out_from(h, d):
        source = (uly + n_uly - d) % n_uly
        src = stage_v.at[h, pl.ds(pl.multiple_of(uly * 64, 64), 64), :]
        dst = out_ref.at[:, pl.ds(pl.multiple_of((source * 3 + h) * 128, 128), 128)]
        return remote(src, dst, out_send.at[h, d - 1], out_recv.at[h, d - 1], (cfg, source, blk))

    def own_copy(h):
        src = stage_v.at[h, pl.ds(pl.multiple_of(uly * 64, 64), 64), :]
        dst = out_ref.at[:, pl.ds(pl.multiple_of((uly * 3 + h) * 128, 128), 128)]
        return pltpu.make_async_copy(src, dst, own_sem.at[h])

    for h in range(3):
        numer = acc_v[h] + attend(h, (n_uly - 1) % 2)
        mean_x = numer / numer[:, 64:65]
        high, low = split_bf16(mean_x)
        result = mm(jnp.concatenate([high, high], axis=1), sv_v[h]) + mm(low, sv_v[h, 0:128])
        stage_v[h] = result.astype(BF16)
        for d in range(1, n_uly):
            out_copy(h, d).start()
        own_copy(h).start()

    vel_done = []
    for copy in blk_copies + uly_copies:
        copy.wait_send()
    for d in range(1, n_x):
        x_copy(d, uly).wait_send()
    sib_copy(0, uly).wait_send()
    for d in range(1, n_x):
        sib_copy(d, x_slot(d)).wait_send()
    for h in range(3):
        own_copy(h).wait()
        for d in range(1, n_uly):
            out_copy(h, d).wait_send()
            out_from(h, d).wait_recv()


def solution(mesh):
    n_uly = mesh.shape["uly"]
    n_blk = mesh.shape["blk"]
    tables = rope_tables()

    def on_device(
        hidden, final_mod, final_weight, latent, guidance, step_size, step_index, embed_weight, block_mod, qkv_weight, qk_gains
    ):
        smem = pl.BlockSpec(memory_space=pltpu.SMEM)
        vmem = pl.BlockSpec(memory_space=pltpu.VMEM)
        anywhere = pl.BlockSpec(memory_space=pl.ANY)
        rows, width = hidden.shape[1:]
        cols = qkv_weight.shape[2]
        heads = cols // HEAD_DIM
        keys = GRID_H * GRID_W
        queries = rows * n_uly
        dma = pltpu.SemaphoreType.DMA
        next_latent, attention = pl.pallas_call(
            functools.partial(kernel, n_uly, n_blk),
            out_shape=(
                jax.ShapeDtypeStruct((rows, CHAN), F32),
                jax.ShapeDtypeStruct((rows, width), BF16),
            ),
            in_specs=[smem] * 3 + [anywhere] * 7 + [vmem] + [anywhere] * 4,
            out_specs=(vmem, anywhere),
            scratch_shapes=[
                pltpu.VMEM((rows, width), BF16),
                pltpu.VMEM((2, width), F32),
                pltpu.VMEM((CHAN, width), BF16),
                pltpu.VMEM((rows, CHAN), F32),
                pltpu.VMEM((CHAN, width), F32),
                pltpu.VMEM((2, width), F32),
                pltpu.VMEM((3, width, cols), BF16),
                pltpu.VMEM(tables[0].shape, F32),
                pltpu.VMEM(tables[1].shape, F32),
                pltpu.VMEM(tables[2].shape[1:], F32),
                pltpu.VMEM(tables[3].shape, F32),
                pltpu.VMEM((32, 128), F32),
                pltpu.VMEM((32, 128), F32),
                pltpu.VMEM((n_uly, n_blk * 32, 128), BF16),
                pltpu.VMEM((n_uly, 32, 128), BF16),
                pltpu.VMEM((144, width), BF16),
                pltpu.VMEM((cols, 256), BF16),
                pltpu.VMEM((cols, 256), BF16),
                pltpu.VMEM((heads, 256, 128), BF16),
                pltpu.VMEM((4, 64, keys), F32),
                pltpu.VMEM((2, keys, 128), BF16),
                pltpu.VMEM((2, heads, 128, keys), BF16),
                pltpu.VMEM((heads, queries, 128), BF16),
                pltpu.VMEM((heads, queries, 128), F32),
                pltpu.VMEM((heads, queries, 128), BF16),
                dma((13,)),
                dma,
                dma,
                dma((n_blk - 1,)),
                dma((n_blk - 1,)),
                dma((n_uly - 1,)),
                dma((n_uly - 1,)),
                dma((n_uly // 2 - 1,)),
                dma((n_uly // 2 - 1,)),
                dma((n_uly // 2,)),
                dma((n_uly // 2,)),
                dma((heads, n_uly - 1)),
                dma((heads, n_uly - 1)),
                dma((heads,)),
            ],
            compiler_params=pltpu.CompilerParams(
                collective_id=0, has_side_effects=True, vmem_limit_bytes=56 << 20
            ),
        )(
            guidance,
            step_size,
            step_index,
            hidden[0],
            final_mod[0],
            final_weight.T,
            latent,
            embed_weight,
            block_mod[0],
            jnp.transpose(qkv_weight, (1, 0, 2)),
            qk_gains,
            *[jnp.asarray(t) for t in tables],
        )
        return (next_latent, attention[None])

    return jax.shard_map(
        on_device,
        mesh=mesh,
        in_specs=(
            P("cfg", ("uly", "blk"), None),
            P("cfg", None, None),
            P(),
            P(("uly", "blk"), None),
            P(),
            P(),
            P(),
            P(),
            P("cfg", None, None),
            P(None, None, "uly"),
            P(),
        ),
        out_specs=(P(("uly", "blk"), None), P("cfg", ("uly", "blk"), None)),
        check_vma=False,
    )
```

time: 374 us -> 53.8 us (0.14)
  waiting for transfers between devices: 174 us -> 0 us
  matrix products: 79.8 us -> 0 us
  local copies, waits for them, and re-layouts: 68.5 us -> 3.14 us
  Pallas kernels: 0 us -> 49.2 us
  other arithmetic: 16.8 us -> 0 us
  between operations: 15 us -> 1.29 us
  blocking collectives: 12.8 us -> 0 us
  starting transfers between devices: 4.09 us -> 0 us
    all_gather x2 -> x0, waiting for transfers between devices: 174 us -> none  [the longest x1 142 us: on_device(): piece = lax.all_gather(key_values, 'blk', axis=0, tiled=True)]
    dot_general x35 -> x0, matrix products: 79.8 us -> none  [the longest x16 44.7 us: attend_block(): jnp.einsum('hqk,khd->qhd', weights.astype(jnp.bfloat16), values, preferre...]
    pallas_call x0 -> x1, Pallas kernels: none -> 49.2 us  [on_device(): pl.pallas_call(functools.partial(kernel, n_uly, n_blk), out_shape=(jax.Sh...]
    squeeze x18 -> x0, local copies, waits for them, and re-layouts: 34.7 us -> none  [the longest x16 33.8 us: on_device(): carry, unused = lax.scan(step_block, carry, blocks)]
    unnamed x11 -> x2, local copies, waits for them, and re-layouts: 31.3 us -> 3.14 us
    all_to_all x1 -> x0, blocking collectives: 12.8 us -> none  [on_device(): lax.all_to_all(result, 'uly', split_axis=0, concat_axis=1, tiled=True)]
    another operation x4 -> x0, other arithmetic: 4.87 us -> none
    reduce_sum x5 -> x0, other arithmetic: 4.31 us -> none  [the longest x2 1.52 us: layer_norm(): var = jnp.mean(centred * centred, axis=-1, keepdims=True)]
  transfers between devices with their start and end apart: 3 -> 0, of which waited for: 2 -> 0; matrix products, arithmetic and copies ran while one was open for 1% -> 0% of each run, Pallas kernels for 0% -> 0%
where the time goes in v1:
time: 53.8 us; the launch traced here: 53.6 us
  Pallas kernels  49.2 us (91%)
  local copies, waits for them, and re-layouts  3.14 us (6%)
  between operations  1.29 us (2%)
    pallas_call x1, Pallas kernels, on_device(): pl.pallas_call(functools.partial(kernel, n_uly, n_blk), out_shape=(jax.Sh...  49.2 us
    unnamed x2, local copies, waits for them, and re-layouts  3.14 us

profile of v1, /device:TPU:1, one launch (start us, length us, event | category | flops | bytes accessed | tf_op | source)
XLA Modules:
  0.0 53.6 jit_solution(15576678268212091321)
XLA Ops:
  1.3 49.2 %shard_map.158 = (f32[64,64]{1,0:T(8,128)}, bf16[64,3072]{1,0:T(8,128)(2,1)}) custom-call(f32[50]{0:T(128)} %guid_s.1, f32[50]{0:T(128)} %size_s.1, s32[1]{0:T(128)S(6)} %copy.19.index_s, bf16[64,3072]{1,0:T(8,128)(2,1)} %bitcast.7, f32[2,3072]{1,0:T(2,128)} %bitcast.10, bf16[64,3072]{1,0:T(8,128)(2,1)} %bitcast.8, f32[64,64]{1,0:T(8,128)} %latent_h.1, ...), custom_call_target="tpu_custom_call" | custom-call | tf_op jit(solution)/shard_map/pallas_call | solution.py:450
  50.5 1.4 %copy.20 = f32[64,64]{1,0:T(8,128)} copy(f32[64,64]{1,0:T(8,128)} %get-tuple-element.8) | data formatting | bytes 32768
  51.8 1.8 %copy.21 = bf16[1,64,3072]{2,1,0:T(8,128)(2,1)} copy(bf16[1,64,3072]{2,1,0:T(8,128)(2,1)} %bitcast.9) | data formatting | bytes 786432

commit v2 on v1

v2 whole, which is shorter than its diff:
```python
import functools
import math

import jax
import jax.numpy as jnp
import numpy as np
from jax import lax
from jax.experimental import pallas as pl
from jax.experimental.pallas import tpu as pltpu
from jax.sharding import PartitionSpec as P

HEAD_DIM = 128
GRID_H = 32
GRID_W = 32
CHAN = 64
EPS = 1e-6
MESH = pl.DeviceIdType.MESH
F32 = jnp.float32
BF16 = jnp.bfloat16


def pair_angles():
    time_dim = HEAD_DIM // 8
    space_dim = (HEAD_DIM - time_dim) // 2
    out = []
    for coords, width in ((8, time_dim), (GRID_H, space_dim), (GRID_W, space_dim)):
        freqs = 1.0 / 256.0 ** (np.arange(0, width, 2) / width)
        out.append(np.arange(coords)[:, None] * freqs[None, :])
    return out


def rope_tables(n_uly, n_y, n_z):
    time, row, col = pair_angles()
    n_x = n_uly // 2
    key = np.zeros((n_z, 2, 64, 2, n_y, GRID_W))
    query = np.zeros((n_y * n_z, 64, 2, 2, GRID_W))
    for half in range(2):
        for y in range(n_y):
            for z in range(n_z):
                at = row[2 * (y * n_z + z) + half]
                key[z, half, 8:36, :, y] = at[:, None, None]
                key[z, half, 36:64, :, y] = col.T[:, None]
                query[y * n_z + z, 8:36, :, half] = at[:, None, None]
                query[y * n_z + z, 36:64, :, half] = col.T[:, None]
    key = key.reshape(n_z, 2, 64, 128)
    query = query.reshape(n_y * n_z, 64, 128)
    frame = [2 * x + core for core in range(2) for x in range(n_x)]
    key_time = np.repeat(time[frame].T, n_y * GRID_W, axis=1)
    query_time = np.repeat(time.T, 2 * GRID_W, axis=1)

    def both(angles, axis):
        return np.stack([np.cos(angles), np.sin(angles)], axis=axis).astype(np.float32)

    return both(key, 2), both(key_time, 0), both(query, 1), both(query_time, 0)


def mm(a, b):
    return jnp.dot(a, b, preferred_element_type=F32)


def mm_nt(a, b, precision=None):
    return lax.dot_general(a, b, (((1,), (1,)), ((), ())), precision=precision, preferred_element_type=F32)


def split_bf16(value):
    high = value.astype(BF16)
    return high, (value - high.astype(F32)).astype(BF16)


def kernel(
    n_uly,
    n_y,
    n_z,
    guid_s,
    size_s,
    index_s,
    hidden_h,
    fmod_h,
    fw_h,
    latent_h,
    embed_h,
    bmod_h,
    w_h,
    gains_v,
    ktab_h,
    ktime_h,
    qtab_h,
    qtime_h,
    next_ref,
    out_ref,
    hidden_v,
    fmod_v,
    fw_v,
    latent_v,
    embed_v,
    bmod_v,
    w_v,
    ktab_v,
    ktime_v,
    qtab_v,
    qtime_v,
    vel_mine,
    vel_other,
    xp_v,
    lhs_v,
    tk_v,
    tq_v,
    sv_v,
    aug_v,
    kt_v,
    q_v,
    acc_v,
    stage_v,
    load_sem,
    vel_send,
    vel_recv,
    plane_send,
    plane_recv,
    z_send,
    z_recv,
    group_send,
    group_recv,
    sib_send,
    sib_recv,
    out_send,
    out_recv,
    own_sem,
):
    cfg = lax.axis_index("cfg")
    uly = lax.axis_index("uly")
    blk = lax.axis_index("blk")
    x_at = uly // 2
    core = uly % 2
    sib = uly + 1 - 2 * core
    y_at = blk // n_z
    z_at = blk % n_z
    n_x = n_uly // 2
    half_rows = n_x * n_y * 32

    def remote(src, dst, send, recv, device):
        return pltpu.make_async_remote_copy(
            src_ref=src, dst_ref=dst, send_sem=send, recv_sem=recv, device_id=device, device_id_type=MESH
        )

    def near(dx, dy, dc):
        return (cfg, (x_at + dx) % n_x * 2 + (core + dc) % 2, (y_at + dy) % n_y * n_z + z_at)

    def ahead(off):
        return (cfg, uly, y_at * n_z + (z_at + n_z + off) % n_z)

    plane = [(dx, dy, dc) for dx in (2, 1, 3, 0) for dy in (1, 0) for dc in (1, 0) if dx + dy + dc > 0]
    side = [(dx, dy, 0) for dx in (2, 1, 3, 0) for dy in (1, 0) if dx + dy > 0]
    groups = [(1, 2), (3, n_z - 1)]
    leave = (2, 1, 3, 0)

    pairs = [
        (hidden_h, hidden_v),
        (fmod_h, fmod_v),
        (fw_h, fw_v),
        (latent_h, latent_v),
        (embed_h, embed_v),
        (bmod_h, bmod_v),
        (w_h.at[0], w_v.at[0]),
        (w_h.at[1], w_v.at[1]),
        (w_h.at[2], w_v.at[2]),
        (ktab_h, ktab_v),
        (ktime_h, ktime_v),
        (qtab_h.at[blk], qtab_v),
        (qtime_h, qtime_v),
    ]
    loads = [pltpu.make_async_copy(s, d, load_sem.at[i]) for i, (s, d) in enumerate(pairs)]
    for load in loads[:4]:
        load.start()

    barrier = pltpu.get_barrier_semaphore()
    for off in range(1, n_z):
        pl.semaphore_signal(barrier, inc=1, device_id=ahead(off), device_id_type=MESH)
    for offs in plane:
        pl.semaphore_signal(barrier, inc=1, device_id=near(*offs), device_id_type=MESH)
    pl.semaphore_signal(barrier, inc=1, device_id=(1 - cfg, uly, blk), device_id_type=MESH)

    for i in range(3):
        loads[i].wait()
    for load in loads[4:]:
        load.start()
    rows = hidden_v[...].astype(F32)
    mean = jnp.mean(rows, axis=1, keepdims=True)
    rows = rows - mean
    var = jnp.mean(rows * rows, axis=1, keepdims=True)
    rows = rows * lax.rsqrt(var + EPS)
    rows = (rows * (1.0 + fmod_v[1:2, :]) + fmod_v[0:1, :]).astype(BF16)
    vel = mm_nt(rows, fw_v[...])
    vel_mine[...] = jnp.concatenate([vel[0:32], vel[32:64]], axis=1)

    pl.semaphore_wait(barrier, len(plane) + n_z)
    vel_copy = remote(vel_mine, vel_other, vel_send, vel_recv, (1 - cfg, uly, blk))
    vel_copy.start()

    loads[3].wait()
    loads[4].wait()
    loads[5].wait()
    emb = embed_v[...]
    emb = emb - jnp.mean(emb, axis=1, keepdims=True)
    high, low = split_bf16(emb)
    stack = jnp.concatenate([high, low], axis=0)
    gram = mm_nt(stack, stack)
    gram = (gram[0:64, 0:64] + gram[0:64, 64:128] + gram[64:128, 0:64] + gram[64:128, 64:128]) * (1.0 / emb.shape[1])
    high, low = split_bf16(emb * (1.0 + bmod_v[1:2, :]))
    lhs_v[0:64, :] = high
    lhs_v[64:128, :] = low
    high, low = split_bf16(bmod_v[0:1, :])
    lhs_v[128:144, :] = jnp.concatenate([high, low, jnp.zeros((14, high.shape[1]), BF16)], axis=0)

    step = index_s[0]
    scale_now = guid_s[step]
    step_now = size_s[step]
    vel_copy.wait()
    mine = vel_mine[...]
    other = vel_other[...]
    cond = jnp.where(cfg == 0, mine, other)
    uncond = jnp.where(cfg == 0, other, mine)
    guided = uncond + scale_now * (cond - uncond)
    guided = jnp.concatenate([guided[:, 0:64], guided[:, 64:128]], axis=0)
    latent = latent_v[...] - step_now * guided
    next_ref[...] = latent
    power = jnp.dot(latent, gram, precision=lax.Precision.HIGHEST, preferred_element_type=F32)
    var = jnp.maximum(jnp.sum(power * latent, axis=1, keepdims=True), 0.0)
    normed = (latent * lax.rsqrt(var + EPS)).astype(BF16)
    own_at = ((core * n_x + x_at) * n_y + y_at) * 32
    own_rows = pl.ds(pl.multiple_of(own_at, 32), 32)
    own_half = pl.ds(pl.multiple_of(core * half_rows, half_rows), half_rows)
    sib_half = pl.ds(pl.multiple_of((1 - core) * half_rows, half_rows), half_rows)
    xp_v[0, own_rows, :] = jnp.concatenate([normed[0:32], normed[32:64]], axis=1)

    def rows_of(dx, dy, dc):
        at = ((core + dc) % 2 * n_x + (x_at + n_x - dx) % n_x) * n_y + (y_at + dy) % n_y
        return pl.ds(pl.multiple_of(at * 32, 32), 32)

    def offset(r):
        return (r + 1) // 2 * (2 * (r % 2) - 1)

    def z_copy(r):
        src = xp_v.at[0, own_rows, :]
        dst = xp_v.at[r, own_rows, :]
        return remote(src, dst, z_send.at[r - 1], z_recv.at[r - 1], ahead(-offset(r)))

    def plane_copy(k):
        there = xp_v.at[0, own_rows, :]
        return remote(there, there, plane_send.at[k], plane_recv.at[k], near(*plane[k]))

    def plane_from(k):
        there = xp_v.at[0, rows_of(*plane[k]), :]
        return remote(there, there, plane_send.at[k], plane_recv.at[k], near(*plane[k]))

    def group_copy(g, k):
        first, last = groups[g]
        there = xp_v.at[first : last + 1, own_rows, :]
        return remote(there, there, group_send.at[g, k], group_recv.at[g, k], near(*side[k]))

    def group_from(g, k):
        first, last = groups[g]
        there = xp_v.at[first : last + 1, rows_of(*side[k]), :]
        return remote(there, there, group_send.at[g, k], group_recv.at[g, k], near(*side[k]))

    def sib_copy(g):
        first, last = groups[g]
        there = xp_v.at[first : last + 1, own_half, :]
        return remote(there, there, sib_send.at[g], sib_recv.at[g], (cfg, sib, blk))

    def sib_from(g):
        first, last = groups[g]
        there = xp_v.at[first : last + 1, sib_half, :]
        return remote(there, there, sib_send.at[g], sib_recv.at[g], (cfg, sib, blk))

    def spread(g):
        first, last = groups[g]
        for r in range(first, last + 1):
            z_copy(r).wait_recv()
        for k in range(len(side)):
            group_copy(g, k).start()

    def share(g):
        for k in range(len(side)):
            group_from(g, k).wait_recv()
        sib_copy(g).start()

    for r in range(1, 3):
        z_copy(r).start()
    for k in range(len(plane)):
        plane_copy(k).start()
    for r in range(3, n_z):
        z_copy(r).start()

    lanes = lax.broadcasted_iota(jnp.int32, (128, 128), 1)
    sublanes = lax.broadcasted_iota(jnp.int32, (128, 128), 0)
    source = jnp.where(sublanes < 64, 2 * sublanes, 2 * sublanes - 127)
    perm = jnp.where(lanes == source, 1.0, 0.0)
    perm_b = perm.astype(BF16)
    lhs = lhs_v[...]
    for j in range(3):
        loads[6 + j].wait()
        full = mm(lhs, w_v[j])
        weight = full[0:64] + full[64:128]
        bias = full[128:129] + full[129:130]
        square = jnp.concatenate([weight, bias, jnp.zeros((63, weight.shape[1]), F32)], axis=0)
        high, low = split_bf16(square)
        for h in range(3):
            cols = slice(h * 128, h * 128 + 128)
            if j == 2:
                sv_v[h, 0:128, :] = high[:, cols]
                sv_v[h, 128:256, :] = low[:, cols]
            else:
                target = tq_v if j == 0 else tk_v
                target[cols, 0:128] = mm_nt(perm_b, high[:, cols]).astype(BF16)
                target[cols, 128:256] = mm_nt(perm_b, low[:, cols]).astype(BF16)

    for i in range(9, 13):
        loads[i].wait()
    gains = jnp.concatenate([gains_v[...], jnp.zeros((6, 128), F32)], axis=0)
    gains = mm_nt(perm, gains, precision=lax.Precision.HIGHEST)
    ga_q = gains[0:64, 0:1] * (math.log2(math.e) / math.sqrt(HEAD_DIM))
    gb_q = gains[64:128, 0:1] * (math.log2(math.e) / math.sqrt(HEAD_DIM))
    ga_k = gains[0:64, 1:2]
    gb_k = gains[64:128, 1:2]

    one_hot = jnp.where(lax.broadcasted_iota(jnp.int32, (1, 128), 1) == 64, 1.0, 0.0)
    low_lanes = lax.broadcasted_iota(jnp.int32, (1, 128), 1) < 64

    def unpack(value):
        wide = value.astype(F32)
        first = jnp.where(low_lanes, wide, one_hot).astype(BF16)
        second = jnp.where(low_lanes, pltpu.roll(wide, 64, 1), one_hot).astype(BF16)
        return first, second

    def rope_tabs(ga, gb, cosine, sine):
        return ga * cosine, gb * sine, ga * sine, gb * cosine

    def rotate(proj, t1, t2, t3, t4):
        a, b = proj[0:64], proj[64:128]
        power = jnp.sum(a * a + b * b, axis=0, keepdims=True) * (1.0 / HEAD_DIM)
        scale = lax.rsqrt(power + EPS)
        return (a * t1 - b * t2) * scale, (a * t3 + b * t4) * scale

    def laid(time, rest, times):
        return jnp.concatenate([time, jnp.concatenate([rest] * times, axis=1)], axis=0)

    def make_keys(r):
        halves = unpack(xp_v[r])
        at = (z_at + n_z + offset(r)) % n_z
        size = 2 * half_rows
        times = rope_tabs(ga_k[0:8], gb_k[0:8], ktime_v[0], ktime_v[1])
        for half in range(2):
            cols = slice(half * size, half * size + size)
            aug_v[r, cols, :] = halves[half]
            proj = mm_nt(tk_v[...], jnp.concatenate([halves[half]] * 2, axis=1))
            rests = rope_tabs(ga_k[8:64], gb_k[8:64], ktab_v[at, half, 0, 8:64], ktab_v[at, half, 1, 8:64])
            tabs = [laid(t, r, size // 128) for t, r in zip(times, rests)]
            for h in range(3):
                ka, kb = rotate(proj[h * 128 : h * 128 + 128], *tabs)
                kt_v[r, h, 0:64, cols] = ka.astype(BF16)
                kt_v[r, h, 64:128, cols] = kb.astype(BF16)

    def attend(h, r, rows=slice(None)):
        scores = mm(q_v[h, rows], kt_v[r, h])
        return mm(jnp.exp2(scores).astype(BF16), aug_v[r])

    spread(0)
    for k in range(len(plane)):
        plane_from(k).wait_recv()

    parts = []
    for dx in leave:
        for c in range(2):
            at = (c * n_x + (x_at + dx) % n_x) * n_y + y_at
            parts += list(unpack(xp_v[0, pl.ds(pl.multiple_of(at * 32, 32), 32), :]))
    rows_q = jnp.concatenate(parts, axis=0)
    proj = mm_nt(tq_v[...], jnp.concatenate([rows_q, rows_q], axis=1))
    here = [pl.ds(pl.multiple_of((x_at + dx) % n_x * 128, 128), 128) for dx in leave]
    cos_t, sin_t = [jnp.concatenate([qtime_v[i, :, lanes] for lanes in here], axis=1) for i in range(2)]
    times = rope_tabs(ga_q[0:8], gb_q[0:8], cos_t, sin_t)
    rests = rope_tabs(ga_q[8:64], gb_q[8:64], qtab_v[0, 8:64], qtab_v[1, 8:64])
    tabs = [laid(t, r, n_uly * 64 // 128) for t, r in zip(times, rests)]
    for h in range(3):
        qa, qb = rotate(proj[h * 128 : h * 128 + 128], *tabs)
        q_v[h] = jnp.transpose(jnp.concatenate([qa, qb], axis=0)).astype(BF16)

    make_keys(0)
    acc_v[0] = attend(0, 0)
    spread(1)
    acc_v[1] = attend(1, 0)
    share(0)
    acc_v[2] = attend(2, 0)
    sib_from(0).wait_recv()

    make_keys(1)
    for h in range(2):
        acc_v[h] += attend(h, 1)
    share(1)
    make_keys(2)
    acc_v[2] += attend(2, 1)
    for h in range(3):
        acc_v[h] += attend(h, 2)
    sib_from(1).wait_recv()
    make_keys(3)
    for h in range(3):
        acc_v[h] += attend(h, 3)
    for r in range(4, n_z):
        make_keys(r)

    width = 3 * HEAD_DIM

    def out_copy(j, dc, h=None):
        c = (core + dc) % 2
        rows = pl.ds(pl.multiple_of(j * 128 + c * 64, 64), 64)
        first, size = (0, width) if h is None else (h * 128, 128)
        src = stage_v.at[rows, first : first + size]
        dst = out_ref.at[:, pl.ds(pl.multiple_of(uly * width + first, 128), size)]
        if leave[j] + dc == 0:
            return pltpu.make_async_copy(src, dst, own_sem)
        to = (x_at + leave[j]) % n_x * 2 + c
        sem = (h or 0, j, dc)
        return remote(src, dst, out_send.at[sem], out_recv.at[sem], (cfg, to, blk))

    def out_from(j, dc, h=None):
        source = (x_at + n_x - leave[j]) % n_x * 2 + (core + dc) % 2
        first, size = (0, width) if h is None else (h * 128, 128)
        src = stage_v.at[0:64, first : first + size]
        dst = out_ref.at[:, pl.ds(pl.multiple_of(source * width + first, 128), size)]
        sem = (h or 0, j, dc)
        return remote(src, dst, out_send.at[sem], out_recv.at[sem], (cfg, source, blk))

    sends = [(0, 0, None), (0, 1, None), (1, 0, None), (1, 1, None)]
    sends += [(2, dc, h) for h in range(3) for dc in range(2)] + [(3, 1, None)]
    for half in range(2):
        rows = slice(half * 256, half * 256 + 256)
        for h in range(3):
            numer = acc_v[h, rows]
            for r in range(4, n_z):
                numer += attend(h, r, rows)
            mean_x = numer / numer[:, 64:65]
            high, low = split_bf16(mean_x)
            result = mm(jnp.concatenate([high, high], axis=1), sv_v[h]) + mm(low, sv_v[h, 0:128])
            stage_v[rows, h * 128 : h * 128 + 128] = result.astype(BF16)
            if half == 1:
                for dc in (1, 0):
                    out_copy(2, dc, h).start()
        for j in ((0, 1), (3,))[half]:
            for dc in (1, 0):
                out_copy(j, dc).start()

    for k in range(len(plane)):
        plane_copy(k).wait_send()
    for r in range(1, n_z):
        z_copy(r).wait_send()
    for g in range(len(groups)):
        for k in range(len(side)):
            group_copy(g, k).wait_send()
        sib_copy(g).wait_send()
    out_copy(3, 0).wait()
    for j, dc, h in sends:
        out_copy(j, dc, h).wait_send()
        out_from(j, dc, h).wait_recv()


def hand_over(next_in, out_in, next_ref, out_ref):
    next_ref[...] = next_in[...]
    out_ref[...] = out_in[...]


def solution(mesh):
    n_uly = mesh.shape["uly"]
    n_blk = mesh.shape["blk"]
    n_y = 2
    n_z = n_blk // n_y
    tables = rope_tables(n_uly, n_y, n_z)

    def on_device(
        hidden, final_mod, final_weight, latent, guidance, step_size, step_index, embed_weight, block_mod, qkv_weight, qk_gains
    ):
        smem = pl.BlockSpec(memory_space=pltpu.SMEM)
        vmem = pl.BlockSpec(memory_space=pltpu.VMEM)
        anywhere = pl.BlockSpec(memory_space=pl.ANY)
        rows, width = hidden.shape[1:]
        cols = qkv_weight.shape[2]
        heads = cols // HEAD_DIM
        keys = 64 * n_uly * n_y
        queries = rows * n_uly
        dma = pltpu.SemaphoreType.DMA
        next_latent, attention = pl.pallas_call(
            functools.partial(kernel, n_uly, n_y, n_z),
            out_shape=(
                jax.ShapeDtypeStruct((rows, CHAN), F32),
                jax.ShapeDtypeStruct((rows, width), BF16),
            ),
            in_specs=[smem] * 3 + [anywhere] * 7 + [vmem] + [anywhere] * 4,
            out_specs=(vmem, anywhere),
            scratch_shapes=[
                pltpu.VMEM((rows, width), BF16),
                pltpu.VMEM((2, width), F32),
                pltpu.VMEM((CHAN, width), BF16),
                pltpu.VMEM((rows, CHAN), F32),
                pltpu.VMEM((CHAN, width), F32),
                pltpu.VMEM((2, width), F32),
                pltpu.VMEM((3, width, cols), BF16),
                pltpu.VMEM(tables[0].shape, F32),
                pltpu.VMEM(tables[1].shape, F32),
                pltpu.VMEM(tables[2].shape[1:], F32),
                pltpu.VMEM(tables[3].shape, F32),
                pltpu.VMEM((32, 128), F32),
                pltpu.VMEM((32, 128), F32),
                pltpu.VMEM((n_z, n_uly * n_y * 32, 128), BF16),
                pltpu.VMEM((144, width), BF16),
                pltpu.VMEM((cols, 256), BF16),
                pltpu.VMEM((cols, 256), BF16),
                pltpu.VMEM((heads, 256, 128), BF16),
                pltpu.VMEM((n_z, keys, 128), BF16),
                pltpu.VMEM((n_z, heads, 128, keys), BF16),
                pltpu.VMEM((heads, queries, 128), BF16),
                pltpu.VMEM((heads, queries, 128), F32),
                pltpu.VMEM((queries, cols), BF16),
                dma((13,)),
                dma,
                dma,
                dma((n_uly * n_y - 1,)),
                dma((n_uly * n_y - 1,)),
                dma((n_z - 1,)),
                dma((n_z - 1,)),
                dma((2, n_uly // 2 * n_y - 1)),
                dma((2, n_uly // 2 * n_y - 1)),
                dma((2,)),
                dma((2,)),
                dma((heads, n_uly // 2, 2)),
                dma((heads, n_uly // 2, 2)),
                dma,
            ],
            compiler_params=pltpu.CompilerParams(
                collective_id=0, has_side_effects=True, vmem_limit_bytes=56 << 20
            ),
        )(
            guidance,
            step_size,
            step_index,
            hidden[0],
            final_mod[0],
            final_weight.T,
            latent,
            embed_weight,
            block_mod[0],
            jnp.transpose(qkv_weight, (1, 0, 2)),
            qk_gains,
            *[jnp.asarray(t) for t in tables],
        )
        next_latent, attention = pl.pallas_call(
            hand_over,
            out_shape=(
                jax.ShapeDtypeStruct((rows, CHAN), F32),
                jax.ShapeDtypeStruct((rows, width), BF16),
            ),
            in_specs=[vmem] * 2,
            out_specs=(vmem, vmem),
        )(next_latent, attention)
        return (next_latent, attention[None])

    return jax.shard_map(
        on_device,
        mesh=mesh,
        in_specs=(
            P("cfg", ("uly", "blk"), None),
            P("cfg", None, None),
            P(),
            P(("uly", "blk"), None),
            P(),
            P(),
            P(),
            P(),
            P("cfg", None, None),
            P(None, None, "uly"),
            P(),
        ),
        out_specs=(P(("uly", "blk"), None), P("cfg", ("uly", "blk"), None)),
        check_vma=False,
    )
```

time: 53.8 us -> 50.2 us (0.933)
  local copies, waits for them, and re-layouts: 3.14 us -> 0 us
    unnamed x2 -> x0, local copies, waits for them, and re-layouts: 3.14 us -> none
    pallas_call x1 -> x2, Pallas kernels: 49.2 us -> 48.7 us  [the longest x1 46.9 us: on_device(): pl.pallas_call(functools.partial(kernel, n_uly, n_y, n_z), out_shape=(jax...]
where the time goes in v2:
time: 50.2 us; the launch traced here: 50 us
  Pallas kernels  48.7 us (97%)
  between operations  1.29 us (3%)
    pallas_call x1, Pallas kernels, on_device(): pl.pallas_call(functools.partial(kernel, n_uly, n_y, n_z), out_shape=(jax...  46.9 us
    pallas_call x1, Pallas kernels, on_device(): pl.pallas_call(hand_over, out_shape=(jax.ShapeDtypeStruct((rows, CHAN), F...  1.79 us

profile of v2, /device:TPU:1, one launch (start us, length us, event | category | flops | bytes accessed | tf_op | source)
XLA Modules:
  0.0 50.0 jit_solution(6636848614823818232)
XLA Ops:
  1.3 46.9 %shard_map.158 = (f32[64,64]{1,0:T(8,128)}, bf16[64,3072]{1,0:T(8,128)(2,1)}) custom-call(f32[50]{0:T(128)} %guid_s.1, f32[50]{0:T(128)} %size_s.1, s32[1]{0:T(128)S(6)} %copy.17.index_s, bf16[64,3072]{1,0:T(8,128)(2,1)} %bitcast.7, f32[2,3072]{1,0:T(2,128)} %bitcast.9, bf16[64,3072]{1,0:T(8,128)(2,1)} %bitcast.8, f32[64,64]{1,0:T(8,128)} %latent_h.1, ...), custom_call_target="tpu_custom_call" | custom-call | tf_op jit(solution)/shard_map/pallas_call | solution.py:489
  48.2 1.8 %shard_map.159 = (f32[64,64]{1,0:T(8,128)}, bf16[64,3072]{1,0:T(8,128)(2,1)}) custom-call(f32[64,64]{1,0:T(8,128)} %get-tuple-element.6.next_in, bf16[64,3072]{1,0:T(8,128)(2,1)} %get-tuple-element.7.out_in), custom_call_target="tpu_custom_call" | custom-call | tf_op jit(solution)/shard_map/pallas_call | solution.py:553

commit v3 on v2

--- a/solution.py
+++ b/solution.py
@@ -103,6 +103,7 @@
     vel_other,
     xp_v,
     lhs_v,
+    gram_v,
     tk_v,
     tq_v,
     sv_v,
@@ -192,24 +193,58 @@
     vel = mm_nt(rows, fw_v[...])
     vel_mine[...] = jnp.concatenate([vel[0:32], vel[32:64]], axis=1)
 
+    lanes = lax.broadcasted_iota(jnp.int32, (128, 128), 1)
+    sublanes = lax.broadcasted_iota(jnp.int32, (128, 128), 0)
+    source = jnp.where(sublanes < 64, 2 * sublanes, 2 * sublanes - 127)
+    perm = jnp.where(lanes == source, 1.0, 0.0)
+    perm_b = perm.astype(BF16)
+
+    def prepare():
+        loads[3].wait()
+        loads[4].wait()
+        loads[5].wait()
+        emb = embed_v[...]
+        emb = emb - jnp.mean(emb, axis=1, keepdims=True)
+        high, low = split_bf16(emb)
+        stack = jnp.concatenate([high, low], axis=0)
+        gram = mm_nt(stack, stack)
+        gram_v[...] = (gram[0:64, 0:64] + gram[0:64, 64:128] + gram[64:128, 0:64] + gram[64:128, 64:128]) * (1.0 / emb.shape[1])
+        high, low = split_bf16(emb * (1.0 + bmod_v[1:2, :]))
+        lhs_v[0:64, :] = high
+        lhs_v[64:128, :] = low
+        high, low = split_bf16(bmod_v[0:1, :])
+        lhs_v[128:144, :] = jnp.concatenate([high, low, jnp.zeros((14, high.shape[1]), BF16)], axis=0)
+
+    def project():
+        lhs = lhs_v[...]
+        for j in range(3):
+            loads[6 + j].wait()
+            full = mm(lhs, w_v[j])
+            weight = full[0:64] + full[64:128]
+            bias = full[128:129] + full[129:130]
+            square = jnp.concatenate([weight, bias, jnp.zeros((63, weight.shape[1]), F32)], axis=0)
+            high, low = split_bf16(square)
+            for h in range(3):
+                cols = slice(h * 128, h * 128 + 128)
+                if j == 2:
+                    sv_v[h, 0:128, :] = high[:, cols]
+                    sv_v[h, 128:256, :] = low[:, cols]
+                else:
+                    target = tq_v if j == 0 else tk_v
+                    target[cols, 0:128] = mm_nt(perm_b, high[:, cols]).astype(BF16)
+                    target[cols, 128:256] = mm_nt(perm_b, low[:, cols]).astype(BF16)
+
+    early = z_at < 3
+
+    @pl.when(early)
+    def _():
+        prepare()
+        project()
+
     pl.semaphore_wait(barrier, len(plane) + n_z)
     vel_copy = remote(vel_mine, vel_other, vel_send, vel_recv, (1 - cfg, uly, blk))
     vel_copy.start()
-
-    loads[3].wait()
-    loads[4].wait()
-    loads[5].wait()
-    emb = embed_v[...]
-    emb = emb - jnp.mean(emb, axis=1, keepdims=True)
-    high, low = split_bf16(emb)
-    stack = jnp.concatenate([high, low], axis=0)
-    gram = mm_nt(stack, stack)
-    gram = (gram[0:64, 0:64] + gram[0:64, 64:128] + gram[64:128, 0:64] + gram[64:128, 64:128]) * (1.0 / emb.shape[1])
-    high, low = split_bf16(emb * (1.0 + bmod_v[1:2, :]))
-    lhs_v[0:64, :] = high
-    lhs_v[64:128, :] = low
-    high, low = split_bf16(bmod_v[0:1, :])
-    lhs_v[128:144, :] = jnp.concatenate([high, low, jnp.zeros((14, high.shape[1]), BF16)], axis=0)
+    pl.when(jnp.logical_not(early))(prepare)
 
     step = index_s[0]
     scale_now = guid_s[step]
@@ -223,7 +258,7 @@
     guided = jnp.concatenate([guided[:, 0:64], guided[:, 64:128]], axis=0)
     latent = latent_v[...] - step_now * guided
     next_ref[...] = latent
-    power = jnp.dot(latent, gram, precision=lax.Precision.HIGHEST, preferred_element_type=F32)
+    power = jnp.dot(latent, gram_v[...], precision=lax.Precision.HIGHEST, preferred_element_type=F32)
     var = jnp.maximum(jnp.sum(power * latent, axis=1, keepdims=True), 0.0)
     normed = (latent * lax.rsqrt(var + EPS)).astype(BF16)
     own_at = ((core * n_x + x_at) * n_y + y_at) * 32
@@ -291,28 +326,7 @@
     for r in range(3, n_z):
         z_copy(r).start()
 
-    lanes = lax.broadcasted_iota(jnp.int32, (128, 128), 1)
-    sublanes = lax.broadcasted_iota(jnp.int32, (128, 128), 0)
-    source = jnp.where(sublanes < 64, 2 * sublanes, 2 * sublanes - 127)
-    perm = jnp.where(lanes == source, 1.0, 0.0)
-    perm_b = perm.astype(BF16)
-    lhs = lhs_v[...]
-    for j in range(3):
-        loads[6 + j].wait()
-        full = mm(lhs, w_v[j])
-        weight = full[0:64] + full[64:128]
-        bias = full[128:129] + full[129:130]
-        square = jnp.concatenate([weight, bias, jnp.zeros((63, weight.shape[1]), F32)], axis=0)
-        high, low = split_bf16(square)
-        for h in range(3):
-            cols = slice(h * 128, h * 128 + 128)
-            if j == 2:
-                sv_v[h, 0:128, :] = high[:, cols]
-                sv_v[h, 128:256, :] = low[:, cols]
-            else:
-                target = tq_v if j == 0 else tk_v
-                target[cols, 0:128] = mm_nt(perm_b, high[:, cols]).astype(BF16)
-                target[cols, 128:256] = mm_nt(perm_b, low[:, cols]).astype(BF16)
+    pl.when(jnp.logical_not(early))(project)
 
     for i in range(9, 13):
         loads[i].wait()
@@ -395,10 +409,11 @@
     make_keys(1)
     for h in range(2):
         acc_v[h] += attend(h, 1)
-    share(1)
     make_keys(2)
     acc_v[2] += attend(2, 1)
-    for h in range(3):
+    acc_v[0] += attend(0, 2)
+    share(1)
+    for h in range(1, 3):
         acc_v[h] += attend(h, 2)
     sib_from(1).wait_recv()
     make_keys(3)
@@ -431,22 +446,30 @@
 
     sends = [(0, 0, None), (0, 1, None), (1, 0, None), (1, 1, None)]
     sends += [(2, dc, h) for h in range(3) for dc in range(2)] + [(3, 1, None)]
-    for half in range(2):
-        rows = slice(half * 256, half * 256 + 256)
-        for h in range(3):
-            numer = acc_v[h, rows]
-            for r in range(4, n_z):
-                numer += attend(h, r, rows)
-            mean_x = numer / numer[:, 64:65]
-            high, low = split_bf16(mean_x)
-            result = mm(jnp.concatenate([high, high], axis=1), sv_v[h]) + mm(low, sv_v[h, 0:128])
-            stage_v[rows, h * 128 : h * 128 + 128] = result.astype(BF16)
-            if half == 1:
-                for dc in (1, 0):
-                    out_copy(2, dc, h).start()
-        for j in ((0, 1), (3,))[half]:
-            for dc in (1, 0):
-                out_copy(j, dc).start()
+    def finish(rows, h):
+        numer = acc_v[h, rows]
+        for r in range(4, n_z):
+            numer += attend(h, r, rows)
+        mean_x = numer * (1.0 / numer[:, 64:65])
+        high, low = split_bf16(mean_x)
+        result = mm(jnp.concatenate([high, high], axis=1), sv_v[h]) + mm(low, sv_v[h, 0:128])
+        stage_v[rows, h * 128 : h * 128 + 128] = result.astype(BF16)
+
+    for h in range(3):
+        finish(slice(0, 256), h)
+    for j in range(2):
+        for dc in (1, 0):
+            out_copy(j, dc).start()
+    for h in range(2):
+        finish(slice(256, 512), h)
+        for dc in (1, 0):
+            out_copy(2, dc, h).start()
+    finish(slice(256, 384), 2)
+    for dc in (1, 0):
+        out_copy(2, dc, 2).start()
+    finish(slice(384, 512), 2)
+    for dc in (1, 0):
+        out_copy(3, dc).start()
 
     for k in range(len(plane)):
         plane_copy(k).wait_send()
@@ -488,12 +511,9 @@
         dma = pltpu.SemaphoreType.DMA
         next_latent, attention = pl.pallas_call(
             functools.partial(kernel, n_uly, n_y, n_z),
-            out_shape=(
-                jax.ShapeDtypeStruct((rows, CHAN), F32),
-                jax.ShapeDtypeStruct((rows, width), BF16),
-            ),
+            out_shape=(pltpu.VMEM((rows, CHAN), F32), pltpu.VMEM((rows, width), BF16)),
             in_specs=[smem] * 3 + [anywhere] * 7 + [vmem] + [anywhere] * 4,
-            out_specs=(vmem, anywhere),
+            out_specs=(vmem, vmem),
             scratch_shapes=[
                 pltpu.VMEM((rows, width), BF16),
                 pltpu.VMEM((2, width), F32),
@@ -510,6 +530,7 @@
                 pltpu.VMEM((32, 128), F32),
                 pltpu.VMEM((n_z, n_uly * n_y * 32, 128), BF16),
                 pltpu.VMEM((144, width), BF16),
+                pltpu.VMEM((CHAN, CHAN), F32),
                 pltpu.VMEM((cols, 256), BF16),
                 pltpu.VMEM((cols, 256), BF16),
                 pltpu.VMEM((heads, 256, 128), BF16),

time: 50.2 us -> 49.6 us (0.988)
  Pallas kernels: 48.7 us -> 46.9 us
  local copies, waits for them, and re-layouts: 0 us -> 1.35 us
    pallas_call x1, Pallas kernels: 46.9 us -> 45.1 us  [on_device(): pl.pallas_call(functools.partial(kernel, n_uly, n_y, n_z), out_shape=(plt...]
    unnamed x0 -> x4, local copies, waits for them, and re-layouts: none -> 1.35 us
where the time goes in v3:
time: 49.6 us; the launch traced here: 49.5 us
  Pallas kernels  46.9 us (95%)
  local copies, waits for them, and re-layouts  1.35 us (3%)
  between operations  1.3 us (3%)
    pallas_call x1, Pallas kernels, on_device(): pl.pallas_call(functools.partial(kernel, n_uly, n_y, n_z), out_shape=(plt...  45.1 us
    pallas_call x1, Pallas kernels, on_device(): pl.pallas_call(hand_over, out_shape=(jax.ShapeDtypeStruct((rows, CHAN), F...  1.79 us
    unnamed x4, local copies, waits for them, and re-layouts  1.35 us

profile of v3, /device:TPU:1, one launch (start us, length us, event | category | flops | bytes accessed | tf_op | source)
XLA Modules:
  0.0 49.5 jit_solution(18404986078512864599)
XLA Ops:
  1.3 45.1 %shard_map.158 = (f32[64,64]{1,0:T(8,128)S(1)}, bf16[64,3072]{1,0:T(8,128)(2,1)S(1)}) custom-call(f32[50]{0:T(128)} %guid_s.1, f32[50]{0:T(128)} %size_s.1, s32[1]{0:T(128)S(6)} %copy.17.index_s, bf16[64,3072]{1,0:T(8,128)(2,1)} %bitcast.7, f32[2,3072]{1,0:T(2,128)} %bitcast.9, bf16[64,3072]{1,0:T(8,128)(2,1)} %bitcast.8, f32[64,64]{1,0:T(8,128)} %latent_h.1, ...), custom_call_target="tpu_custom_call" | custom-call | tf_op jit(solution)/shard_map/pallas_call | solution.py:512
  46.3 0.0 copy-start
  46.4 0.7 %copy-done = bf16[64,3072]{1,0:T(8,128)(2,1)} copy-done((bf16[64,3072]{1,0:T(8,128)(2,1)}, bf16[64,3072]{1,0:T(8,128)(2,1)S(1)}, u32[]{:S(2)}) %copy-start) | copy-done | bytes 393240
  47.1 0.0 copy-start.1
  47.1 0.6 %copy-done.1 = f32[64,64]{1,0:T(8,128)} copy-done((f32[64,64]{1,0:T(8,128)}, f32[64,64]{1,0:T(8,128)S(1)}, u32[]{:S(2)}) %copy-start.1) | copy-done | bytes 16408
  47.7 1.8 %shard_map.159 = (f32[64,64]{1,0:T(8,128)}, bf16[64,3072]{1,0:T(8,128)(2,1)}) custom-call(f32[64,64]{1,0:T(8,128)} %copy-done.1, bf16[64,3072]{1,0:T(8,128)(2,1)} %copy-done), custom_call_target="tpu_custom_call" | custom-call | tf_op jit(solution)/shard_map/pallas_call | solution.py:574
Async XLA Ops:
  46.3 0.8 %copy-start = (bf16[64,3072]{1,0:T(8,128)(2,1)}, bf16[64,3072]{1,0:T(8,128)(2,1)S(1)}, u32[]{:S(2)}) copy-start(bf16[64,3072]{1,0:T(8,128)(2,1)S(1)} %get-tuple-element.7.out_in) | copy-start | bytes 1179652
  47.1 0.6 %copy-start.1 = (f32[64,64]{1,0:T(8,128)}, f32[64,64]{1,0:T(8,128)S(1)}, u32[]{:S(2)}) copy-start(f32[64,64]{1,0:T(8,128)S(1)} %get-tuple-element.6.next_in) | copy-start | bytes 49156

commit v4 on v3

--- a/solution.py
+++ b/solution.py
@@ -485,9 +485,15 @@
         out_from(j, dc, h).wait_recv()
 
 
-def hand_over(next_in, out_in, next_ref, out_ref):
-    next_ref[...] = next_in[...]
-    out_ref[...] = out_in[...]
+def hand_over(next_in, out_in, next_ref, out_ref, sems):
+    copies = [
+        pltpu.make_async_copy(out_in, out_ref, sems.at[0]),
+        pltpu.make_async_copy(next_in, next_ref, sems.at[1]),
+    ]
+    for copy in copies:
+        copy.start()
+    for copy in copies:
+        copy.wait()
 
 
 def solution(mesh):
@@ -578,8 +584,12 @@
                 jax.ShapeDtypeStruct((rows, width), BF16),
             ),
             in_specs=[vmem] * 2,
-            out_specs=(vmem, vmem),
-        )(next_latent, attention)
+            out_specs=(anywhere, anywhere),
+            scratch_shapes=[dma((2,))],
+        )(
+            pltpu.with_memory_space_constraint(next_latent, pltpu.VMEM),
+            pltpu.with_memory_space_constraint(attention, pltpu.VMEM),
+        )
         return (next_latent, attention[None])
 
     return jax.shard_map(

time: 49.6 us -> 47.4 us (0.956)
  local copies, waits for them, and re-layouts: 1.35 us -> 0 us
  Pallas kernels: 46.9 us -> 45.8 us
    unnamed x4 -> x0, local copies, waits for them, and re-layouts: 1.35 us -> none
    pallas_call x1, Pallas kernels: 1.79 us -> 0.77 us  [on_device(): pl.pallas_call(hand_over, out_shape=(jax.ShapeDtypeStruct((rows, CHAN), F...]
where the time goes in v4:
time: 47.4 us; the launch traced here: 47.3 us
  Pallas kernels  45.8 us (97%)
  between operations  1.47 us (3%)
    pallas_call x1, Pallas kernels, on_device(): pl.pallas_call(functools.partial(kernel, n_uly, n_y, n_z), out_shape=(plt...  45.1 us

profile of v4, /device:TPU:1, one launch (start us, length us, event | category | flops | bytes accessed | tf_op | source)
XLA Modules:
  0.0 47.3 jit_solution(11807066824747879935)
XLA Ops:
  1.3 45.1 %shard_map.158 = (f32[64,64]{1,0:T(8,128)S(1)}, bf16[64,3072]{1,0:T(8,128)(2,1)S(1)}) custom-call(f32[50]{0:T(128)} %guid_s.1, f32[50]{0:T(128)} %size_s.1, s32[1]{0:T(128)S(6)} %copy.17.index_s, bf16[64,3072]{1,0:T(8,128)(2,1)} %bitcast.7, f32[2,3072]{1,0:T(2,128)} %bitcast.9, bf16[64,3072]{1,0:T(8,128)(2,1)} %bitcast.8, f32[64,64]{1,0:T(8,128)} %latent_h.1, ...), custom_call_target="tpu_custom_call" | custom-call | tf_op jit(solution)/shard_map/pallas_call | solution.py:518
  46.3 0.8 %shard_map.159 = (f32[64,64]{1,0:T(8,128)}, bf16[64,3072]{1,0:T(8,128)(2,1)}) custom-call(f32[64,64]{1,0:T(8,128)S(1)} %get-tuple-element.6.next_in, bf16[64,3072]{1,0:T(8,128)(2,1)S(1)} %get-tuple-element.7.out_in), custom_call_target="tpu_custom_call" | custom-call | tf_op jit(solution)/shard_map/pallas_call | solution.py:580

commit v5 on v4

--- a/solution.py
+++ b/solution.py
@@ -126,6 +126,7 @@
     out_send,
     out_recv,
     own_sem,
+    relay,
 ):
     cfg = lax.axis_index("cfg")
     uly = lax.axis_index("uly")
@@ -174,7 +175,7 @@
         load.start()
 
     barrier = pltpu.get_barrier_semaphore()
-    for off in range(1, n_z):
+    for off in (1, -1):
         pl.semaphore_signal(barrier, inc=1, device_id=ahead(off), device_id_type=MESH)
     for offs in plane:
         pl.semaphore_signal(barrier, inc=1, device_id=near(*offs), device_id_type=MESH)
@@ -241,10 +242,22 @@
         prepare()
         project()
 
-    pl.semaphore_wait(barrier, len(plane) + n_z)
+    def tell(level):
+        for off in (1, -1):
+            pl.semaphore_signal(relay.at[level], inc=1, device_id=ahead(off), device_id_type=MESH)
+
+    pl.semaphore_wait(barrier, len(plane) + 3)
+    tell(0)
     vel_copy = remote(vel_mine, vel_other, vel_send, vel_recv, (1 - cfg, uly, blk))
     vel_copy.start()
     pl.when(jnp.logical_not(early))(prepare)
+
+    gains = jnp.concatenate([gains_v[...], jnp.zeros((6, 128), F32)], axis=0)
+    gains = mm_nt(perm, gains, precision=lax.Precision.HIGHEST)
+    ga_q = gains[0:64, 0:1] * (math.log2(math.e) / math.sqrt(HEAD_DIM))
+    gb_q = gains[64:128, 0:1] * (math.log2(math.e) / math.sqrt(HEAD_DIM))
+    ga_k = gains[0:64, 1:2]
+    gb_k = gains[64:128, 1:2]
 
     step = index_s[0]
     scale_now = guid_s[step]
@@ -321,22 +334,21 @@
 
     for r in range(1, 3):
         z_copy(r).start()
+    pl.semaphore_wait(relay.at[0], 2)
+    tell(1)
     for k in range(len(plane)):
         plane_copy(k).start()
-    for r in range(3, n_z):
+    pl.semaphore_wait(relay.at[1], 2)
+    tell(2)
+    for r in range(3, n_z - 1):
         z_copy(r).start()
+    pl.semaphore_wait(relay.at[2], 2)
+    z_copy(n_z - 1).start()
 
     pl.when(jnp.logical_not(early))(project)
 
     for i in range(9, 13):
         loads[i].wait()
-    gains = jnp.concatenate([gains_v[...], jnp.zeros((6, 128), F32)], axis=0)
-    gains = mm_nt(perm, gains, precision=lax.Precision.HIGHEST)
-    ga_q = gains[0:64, 0:1] * (math.log2(math.e) / math.sqrt(HEAD_DIM))
-    gb_q = gains[64:128, 0:1] * (math.log2(math.e) / math.sqrt(HEAD_DIM))
-    ga_k = gains[0:64, 1:2]
-    gb_k = gains[64:128, 1:2]
-
     one_hot = jnp.where(lax.broadcasted_iota(jnp.int32, (1, 128), 1) == 64, 1.0, 0.0)
     low_lanes = lax.broadcasted_iota(jnp.int32, (1, 128), 1) < 64
 
@@ -559,6 +571,7 @@
                 dma((heads, n_uly // 2, 2)),
                 dma((heads, n_uly // 2, 2)),
                 dma,
+                pltpu.SemaphoreType.REGULAR((n_z // 2 - 1,)),
             ],
             compiler_params=pltpu.CompilerParams(
                 collective_id=0, has_side_effects=True, vmem_limit_bytes=56 << 20

time: 47.4 us -> 48.6 us (1.025)
  Pallas kernels: 45.8 us -> 47 us
    pallas_call x1, Pallas kernels: 45.1 us -> 46.2 us  [on_device(): pl.pallas_call(functools.partial(kernel, n_uly, n_y, n_z), out_shape=(plt...]
where the time goes in v5:
time: 48.6 us; the launch traced here: 48.4 us
  Pallas kernels  47 us (97%)
  between operations  1.47 us (3%)
    pallas_call x1, Pallas kernels, on_device(): pl.pallas_call(functools.partial(kernel, n_uly, n_y, n_z), out_shape=(plt...  46.2 us

profile of v5, /device:TPU:1, one launch (start us, length us, event | category | flops | bytes accessed | tf_op | source)
XLA Modules:
  0.0 48.4 jit_solution(7038703418494964327)
XLA Ops:
  1.3 46.2 %shard_map.158 = (f32[64,64]{1,0:T(8,128)S(1)}, bf16[64,3072]{1,0:T(8,128)(2,1)S(1)}) custom-call(f32[50]{0:T(128)} %guid_s.1, f32[50]{0:T(128)} %size_s.1, s32[1]{0:T(128)S(6)} %copy.17.index_s, bf16[64,3072]{1,0:T(8,128)(2,1)} %bitcast.7, f32[2,3072]{1,0:T(2,128)} %bitcast.9, bf16[64,3072]{1,0:T(8,128)(2,1)} %bitcast.8, f32[64,64]{1,0:T(8,128)} %latent_h.1, ...), custom_call_target="tpu_custom_call" | custom-call | tf_op jit(solution)/shard_map/pallas_call | solution.py:530
  47.5 0.8 %shard_map.159 = (f32[64,64]{1,0:T(8,128)}, bf16[64,3072]{1,0:T(8,128)(2,1)}) custom-call(f32[64,64]{1,0:T(8,128)S(1)} %get-tuple-element.6.next_in, bf16[64,3072]{1,0:T(8,128)(2,1)S(1)} %get-tuple-element.7.out_in), custom_call_target="tpu_custom_call" | custom-call | tf_op jit(solution)/shard_map/pallas_call | solution.py:593
